TPU v7x, 32 devices: a whole 2x2x4 slice. The times are simulated.
32 devices in a mesh: layer: 4 (over x, core), sub: 8 (over z, y).
Axes of the slice: x: 2, y: 2, z: 4, core: 2. Of those that a mesh axis runs over, the one named last changes fastest.
Arguments:
- screens: float32 [4, 7, 2048, 640], P('layer', None, None, 'sub'), may hold values from -4 to 4
- new_columns: float32 [10, 4, 2048, 8], P(None, 'layer'), may hold values from -4 to 4
- col_block: int32 [10, 4], P(None, 'layer'), may hold values from 240 to 319
- shift_x: int32 [10, 4, 6], P(None, 'layer'), may hold values from -40 to 40, as said below
- shift_y: int32 [10, 4, 6], P(None, 'layer'), may hold values from -40 to 40, as said below
- valid: int32 [80, 80], P('layer', 'sub'), may hold values 0 or 1
- recon: bfloat16 [6, 2, 80, 80, 5376], P(None, None, 'layer', 'sub'), may hold values from -0.0234375 to 0.0234375
Outputs:
- slopes: float32 [10, 6, 2, 80, 80], P(None, None, None, 'layer', 'sub')
- commands: float32 [10, 5376], replicated
Inputs may be any that keep to these rules, and one draw needn't show every extreme that they name: `shift_x`: column shifts reach both -40 and 40 in every draw. `shift_y`: row shifts reach both -40 and 40 in every draw.
All inputs are finite; a program needn't handle non-finite values. No bound on the sum of `valid` on one device may be relied on, other than what follows from the above.
Results may differ from a plain program's by a relative error of at most 0.0029.
Values sent between devices are 32-bit elements; how exact they have to be, the bound alone decides.
A program may use at most 192 MiB of HBM per device.

v0:
```python
import math

import jax
import jax.numpy as jnp
from jax import lax
from jax.sharding import PartitionSpec as P

FFT_LEN = 16
ACTS = 5376
HALO = 40
NEW_COLS = 8
PUP = 640
PUP_TURN = 3
ROW0 = 704


def extended_2(block, sides, width):
    for axis, dim in sides:
        count = lax.axis_size(axis)
        forward = [(i, i + 1) for i in range(count - 1)]
        forward.append((count - 1, 0))
        backward = [(target, source) for source, target in forward]
        low = lax.ppermute(
            lax.slice_in_dim(block, block.shape[dim] - width, None, axis=dim), axis, forward
        )
        high = lax.ppermute(lax.slice_in_dim(block, 0, width, axis=dim), axis, backward)
        block = jnp.concatenate([low, block, high], axis=dim)
    return block


def lenslet_slopes(phase, valid, fft_len):
    stars, rows, cols = phase.shape
    subs_r, subs_c = valid.shape
    pix = rows // subs_r
    tiles = phase.reshape(stars, subs_r, pix, subs_c, pix)
    tiles = jnp.transpose(tiles, (2, 4, 0, 1, 3)).reshape(pix, pix, stars * subs_r * subs_c)
    freq = jnp.arange(fft_len).astype(jnp.float32)
    place = jnp.arange(pix).astype(jnp.float32)
    angle = 2.0 * math.pi / fft_len * freq[:, None] * place[None, :]
    cosine = jnp.cos(angle)
    sine = -jnp.sin(angle)
    real_part = jnp.cos(tiles)
    imag_part = jnp.sin(tiles)
    highest = lax.Precision.HIGHEST

    def along_rows(mat, field):
        return jnp.einsum("kn,nms->kms", mat, field, precision=highest)

    def along_cols(field, mat):
        return jnp.einsum("kms,qm->kqs", field, mat, precision=highest)

    first_re = along_rows(cosine, real_part) - along_rows(sine, imag_part)
    first_im = along_rows(cosine, imag_part) + along_rows(sine, real_part)
    spot_re = along_cols(first_re, cosine) - along_cols(first_im, sine)
    spot_im = along_cols(first_re, sine) + along_cols(first_im, cosine)
    power = spot_re * spot_re + spot_im * spot_im
    centred = ((jnp.arange(fft_len) + fft_len // 2) % fft_len - fft_len // 2).astype(jnp.float32)
    total = jnp.sum(power, axis=(0, 1))
    along_x = jnp.sum(power * centred[None, :, None], axis=(0, 1)) / total
    along_y = jnp.sum(power * centred[:, None, None], axis=(0, 1)) / total
    result = jnp.stack([along_x, along_y]).reshape(2, stars, subs_r, subs_c)
    return jnp.transpose(result, (1, 0, 2, 3)) * valid.astype(jnp.float32)[None, None]


def place_columns(strips, fresh, block, owner, width):
    column = block * NEW_COLS
    turn = column // PUP
    start = column % PUP - owner * width
    inside = (start >= 0) & (start < width)
    offset = jnp.clip(start, 0, width - NEW_COLS)
    placed = lax.dynamic_update_slice(strips, fresh[None], (turn, jnp.int32(0), offset))
    return jnp.where(inside, placed, strips)


def cut_window(extended, step_x, step_y, width):
    return lax.dynamic_slice(extended, (HALO + step_y, HALO + step_x), (PUP, width))


def local(screens, new_columns, col_block, shift_x, shift_y, valid, recon):
    width = screens.shape[3]
    owner = lax.axis_index("sub")
    last = lax.axis_size("sub") - 1
    matrix = recon.reshape(-1, ACTS)

    def advance(strips, inputs):
        fresh, blocks, step_x, step_y = inputs
        strips = jax.vmap(lambda s, f, b: place_columns(s, f, b, owner, width))(
            strips, fresh, blocks
        )
        band = strips[:, PUP_TURN - 1 : PUP_TURN + 2, ROW0 - HALO : ROW0 + PUP + HALO, :]
        before = band[:, 0]
        core = band[:, 1]
        after = band[:, 2]
        tail_cols = jnp.where(
            owner == last, before[:, :, width - HALO :], core[:, :, width - HALO :]
        )
        head_cols = jnp.where(owner == 0, after[:, :, :HALO], core[:, :, :HALO])
        rims = jnp.concatenate([head_cols, tail_cols], axis=2)
        padded = extended_2(rims, (("sub", 2),), HALO)
        extended = jnp.concatenate(
            [padded[:, :, :HALO], core, padded[:, :, padded.shape[2] - HALO :]], axis=2
        )
        window = jax.vmap(
            jax.vmap(lambda e, x, y: cut_window(e, x, y, width), in_axes=(None, 0, 0))
        )(extended, step_x, step_y)
        summed = lax.all_to_all(window, "layer", split_axis=2, concat_axis=0, tiled=True)
        phase = jnp.sum(summed, axis=0)
        slopes = lenslet_slopes(phase, valid, FFT_LEN)
        flat = slopes.astype(jnp.bfloat16).reshape(-1)
        partial_cmd = jnp.dot(flat, matrix, preferred_element_type=jnp.float32)
        command = lax.psum(partial_cmd, ("layer", "sub"))
        return (strips, (slopes, command))

    final, (slopes, commands) = lax.scan(
        advance, screens, (new_columns, col_block, shift_x, shift_y)
    )
    return (slopes, commands)


def solution(mesh):
    return jax.shard_map(
        local,
        mesh=mesh,
        in_specs=(
            P("layer", None, None, "sub"),
            P(None, "layer", None, None),
            P(None, "layer"),
            P(None, "layer", None),
            P(None, "layer", None),
            P("layer", "sub"),
            P(None, None, "layer", "sub", None),
        ),
        out_specs=(P(None, None, None, "layer", "sub"), P()),
        check_vma=False,
    )
```

profile of v0, /device:TPU:1, one launch (start us, length us, event | category | flops | bytes accessed | tf_op | source)
XLA Modules:
  0.0 1919.7 jit_solution(4577020330082178476)
XLA Ops:
  0.6 22.5 %copy.99 = bf16[6,2,20,10,5376]{4,3,2,1,0:T(8,128)(2,1)} copy(bf16[6,2,20,10,5376]{4,1,3,2,0:T(2,128)(2,1)} %param.17) | data formatting | bytes 51609600 | tf_op args[6]
  23.1 45.7 %reshape.362 = bf16[2400,5376]{1,0:T(8,128)(2,1)} reshape(bf16[6,2,20,10,5376]{4,3,2,1,0:T(8,128)(2,1)} %copy.99) | data formatting | bytes 51609600 | tf_op jit(solution)/shard_map/reshape | solution.py:83
  75.8 1843.9 %while.21 = (s32[]{:T(128)}, f32[1,7,2048,80]{3,2,1,0:T(8,128)}, f32[10,6,2,20,10]{3,2,4,1,0:T(2,128)}, f32[10,5376]{1,0:T(8,128)}, s32[10,1]{0,1:T(1,128)S(1)},...) while((s32[]{:T(128)}, f32[1,7,2048,80]{3,2,1,0:T(8,128)}, ...), condition=%wide.region_7.8_spmd, body=%wide.region_0.7_spmd.sunk | while | flops 206700464 | bytes 63458884 | solution.py:114
  99.7 13.9 collective-permute-done
  116.0 12.9 while.22
  136.3 23.4 %all-to-all-done = f32[1,6,640,80]{3,0,1,2:T(1,128)S(1)} async-done(((f32[1,6,640,80]{3,0,1,2:T(1,128)}), f32[1,6,640,80]{3,0,1,2:T(1,128)S(1)}, u32[]{:S(2)}, u32[]{:S(2)}) %all-to-all-start) | async-done | bytes 1228832 | tf_op jit(solution)/shard_map/while/body/eval_jaxpr/all_to_all | solution.py:106
  168.7 9.4 copy.148
  185.3 9.4 copy.146
  208.6 10.3 fusion.107
  218.9 39.3 %psum.12 = f32[1,5376]{1,0:T(1,128)S(1)} all-reduce(f32[1,5376]{1,0:T(1,128)S(1)} %fusion.107), channel_id=1, replica_groups=mesh['layer'=4,'sub'=8] {'layer','sub'}, use_global_device_ids=true, to_apply=%region_6.6 | all-reduce | flops 5376 | bytes 43008 | tf_op jit(solution)/shard_map/while/body/eval_jaxpr/psum | solution.py:111
  283.2 14.6 collective-permute-done
  300.8 12.9 while.22
  321.2 23.4 %all-to-all-done = f32[1,6,640,80]{3,0,1,2:T(1,128)S(1)} async-done(((f32[1,6,640,80]{3,0,1,2:T(1,128)}), f32[1,6,640,80]{3,0,1,2:T(1,128)S(1)}, u32[]{:S(2)}, u32[]{:S(2)}) %all-to-all-start) | async-done | bytes 1228832 | tf_op jit(solution)/shard_map/while/body/eval_jaxpr/all_to_all | solution.py:106
  353.5 9.4 copy.148
  370.1 9.4 copy.146
  393.5 10.3 fusion.107
  403.8 38.5 %psum.12 = f32[1,5376]{1,0:T(1,128)S(1)} all-reduce(f32[1,5376]{1,0:T(1,128)S(1)} %fusion.107), channel_id=1, replica_groups=mesh['layer'=4,'sub'=8] {'layer','sub'}, use_global_device_ids=true, to_apply=%region_6.6 | all-reduce | flops 5376 | bytes 43008 | tf_op jit(solution)/shard_map/while/body/eval_jaxpr/psum | solution.py:111
  466.6 15.7 collective-permute-done
  483.8 12.9 while.22
  505.1 23.4 %all-to-all-done = f32[1,6,640,80]{3,0,1,2:T(1,128)S(1)} async-done(((f32[1,6,640,80]{3,0,1,2:T(1,128)}), f32[1,6,640,80]{3,0,1,2:T(1,128)S(1)}, u32[]{:S(2)}, u32[]{:S(2)}) %all-to-all-start) | async-done | bytes 1228832 | tf_op jit(solution)/shard_map/while/body/eval_jaxpr/all_to_all | solution.py:106
  537.5 9.4 copy.148
  577.5 10.3 fusion.107
  587.8 39.5 %psum.12 = f32[1,5376]{1,0:T(1,128)S(1)} all-reduce(f32[1,5376]{1,0:T(1,128)S(1)} %fusion.107), channel_id=1, replica_groups=mesh['layer'=4,'sub'=8] {'layer','sub'}, use_global_device_ids=true, to_apply=%region_6.6 | all-reduce | flops 5376 | bytes 43008 | tf_op jit(solution)/shard_map/while/body/eval_jaxpr/psum | solution.py:111
  651.5 15.2 collective-permute-done
  668.4 12.9 while.22
  690.0 23.4 %all-to-all-done = f32[1,6,640,80]{3,0,1,2:T(1,128)S(1)} async-done(((f32[1,6,640,80]{3,0,1,2:T(1,128)}), f32[1,6,640,80]{3,0,1,2:T(1,128)S(1)}, u32[]{:S(2)}, u32[]{:S(2)}) %all-to-all-start) | async-done | bytes 1228832 | tf_op jit(solution)/shard_map/while/body/eval_jaxpr/all_to_all | solution.py:106
  722.4 9.4 copy.148
  739.0 9.4 copy.146
  762.3 10.3 fusion.107
  772.6 38.0 %psum.12 = f32[1,5376]{1,0:T(1,128)S(1)} all-reduce(f32[1,5376]{1,0:T(1,128)S(1)} %fusion.107), channel_id=1, replica_groups=mesh['layer'=4,'sub'=8] {'layer','sub'}, use_global_device_ids=true, to_apply=%region_6.6 | all-reduce | flops 5376 | bytes 43008 | tf_op jit(solution)/shard_map/while/body/eval_jaxpr/psum | solution.py:111
  834.9 15.4 collective-permute-done
  851.8 12.9 while.22
  873.4 23.4 %all-to-all-done = f32[1,6,640,80]{3,0,1,2:T(1,128)S(1)} async-done(((f32[1,6,640,80]{3,0,1,2:T(1,128)}), f32[1,6,640,80]{3,0,1,2:T(1,128)S(1)}, u32[]{:S(2)}, u32[]{:S(2)}) %all-to-all-start) | async-done | bytes 1228832 | tf_op jit(solution)/shard_map/while/body/eval_jaxpr/all_to_all | solution.py:106
  945.8 10.3 fusion.107
  956.0 39.4 %psum.12 = f32[1,5376]{1,0:T(1,128)S(1)} all-reduce(f32[1,5376]{1,0:T(1,128)S(1)} %fusion.107), channel_id=1, replica_groups=mesh['layer'=4,'sub'=8] {'layer','sub'}, use_global_device_ids=true, to_apply=%region_6.6 | all-reduce | flops 5376 | bytes 43008 | tf_op jit(solution)/shard_map/while/body/eval_jaxpr/psum | solution.py:111
  1020.5 14.6 collective-permute-done
  1038.1 12.9 while.22
  1058.4 23.4 %all-to-all-done = f32[1,6,640,80]{3,0,1,2:T(1,128)S(1)} async-done(((f32[1,6,640,80]{3,0,1,2:T(1,128)}), f32[1,6,640,80]{3,0,1,2:T(1,128)S(1)}, u32[]{:S(2)}, u32[]{:S(2)}) %all-to-all-start) | async-done | bytes 1228832 | tf_op jit(solution)/shard_map/while/body/eval_jaxpr/all_to_all | solution.py:106
  1130.8 10.3 fusion.107
  1141.0 38.2 %psum.12 = f32[1,5376]{1,0:T(1,128)S(1)} all-reduce(f32[1,5376]{1,0:T(1,128)S(1)} %fusion.107), channel_id=1, replica_groups=mesh['layer'=4,'sub'=8] {'layer','sub'}, use_global_device_ids=true, to_apply=%region_6.6 | all-reduce | flops 5376 | bytes 43008 | tf_op jit(solution)/shard_map/while/body/eval_jaxpr/psum | solution.py:111
  1203.6 15.3 collective-permute-done
  1220.4 12.9 while.22
  1242.0 23.4 %all-to-all-done = f32[1,6,640,80]{3,0,1,2:T(1,128)S(1)} async-done(((f32[1,6,640,80]{3,0,1,2:T(1,128)}), f32[1,6,640,80]{3,0,1,2:T(1,128)S(1)}, u32[]{:S(2)}, u32[]{:S(2)}) %all-to-all-start) | async-done | bytes 1228832 | tf_op jit(solution)/shard_map/while/body/eval_jaxpr/all_to_all | solution.py:106
  1314.4 10.3 fusion.107
  1324.6 39.9 %psum.12 = f32[1,5376]{1,0:T(1,128)S(1)} all-reduce(f32[1,5376]{1,0:T(1,128)S(1)} %fusion.107), channel_id=1, replica_groups=mesh['layer'=4,'sub'=8] {'layer','sub'}, use_global_device_ids=true, to_apply=%region_6.6 | all-reduce | flops 5376 | bytes 43008 | tf_op jit(solution)/shard_map/while/body/eval_jaxpr/psum | solution.py:111
  1388.8 15.2 collective-permute-done
  1405.7 12.9 while.22
  1427.3 23.4 %all-to-all-done = f32[1,6,640,80]{3,0,1,2:T(1,128)S(1)} async-done(((f32[1,6,640,80]{3,0,1,2:T(1,128)}), f32[1,6,640,80]{3,0,1,2:T(1,128)S(1)}, u32[]{:S(2)}, u32[]{:S(2)}) %all-to-all-start) | async-done | bytes 1228832 | tf_op jit(solution)/shard_map/while/body/eval_jaxpr/all_to_all | solution.py:106
  1459.6 9.4 copy.148
  1476.2 9.4 copy.146
  1499.6 10.3 fusion.107
  1509.9 38.5 %psum.12 = f32[1,5376]{1,0:T(1,128)S(1)} all-reduce(f32[1,5376]{1,0:T(1,128)S(1)} %fusion.107), channel_id=1, replica_groups=mesh['layer'=4,'sub'=8] {'layer','sub'}, use_global_device_ids=true, to_apply=%region_6.6 | all-reduce | flops 5376 | bytes 43008 | tf_op jit(solution)/shard_map/while/body/eval_jaxpr/psum | solution.py:111
  1572.7 15.4 collective-permute-done
  1589.5 12.9 while.22
  1611.2 23.4 %all-to-all-done = f32[1,6,640,80]{3,0,1,2:T(1,128)S(1)} async-done(((f32[1,6,640,80]{3,0,1,2:T(1,128)}), f32[1,6,640,80]{3,0,1,2:T(1,128)S(1)}, u32[]{:S(2)}, u32[]{:S(2)}) %all-to-all-start) | async-done | bytes 1228832 | tf_op jit(solution)/shard_map/while/body/eval_jaxpr/all_to_all | solution.py:106
  1683.5 10.3 fusion.107
  1693.8 39.0 %psum.12 = f32[1,5376]{1,0:T(1,128)S(1)} all-reduce(f32[1,5376]{1,0:T(1,128)S(1)} %fusion.107), channel_id=1, replica_groups=mesh['layer'=4,'sub'=8] {'layer','sub'}, use_global_device_ids=true, to_apply=%region_6.6 | all-reduce | flops 5376 | bytes 43008 | tf_op jit(solution)/shard_map/while/body/eval_jaxpr/psum | solution.py:111
  1757.1 15.7 collective-permute-done
  1774.3 12.9 while.22
  1795.6 23.4 %all-to-all-done = f32[1,6,640,80]{3,0,1,2:T(1,128)S(1)} async-done(((f32[1,6,640,80]{3,0,1,2:T(1,128)}), f32[1,6,640,80]{3,0,1,2:T(1,128)S(1)}, u32[]{:S(2)}, u32[]{:S(2)}) %all-to-all-start) | async-done | bytes 1228832 | tf_op jit(solution)/shard_map/while/body/eval_jaxpr/all_to_all | solution.py:106
  1828.0 9.4 copy.148
  1844.6 9.4 copy.146
  1868.0 10.3 fusion.107
  1878.2 39.1 %psum.12 = f32[1,5376]{1,0:T(1,128)S(1)} all-reduce(f32[1,5376]{1,0:T(1,128)S(1)} %fusion.107), channel_id=1, replica_groups=mesh['layer'=4,'sub'=8] {'layer','sub'}, use_global_device_ids=true, to_apply=%region_6.6 | all-reduce | flops 5376 | bytes 43008 | tf_op jit(solution)/shard_map/while/body/eval_jaxpr/psum | solution.py:111
  (707 shorter events, 847.1 us)
Async XLA Ops:
  68.8 6.8 copy-start.2
  68.8 6.8 copy-start.3
  68.8 6.9 copy-start.4
  68.8 7.0 copy-start
  68.8 7.0 copy-start.1
  68.9 6.9 copy-start.5
  95.3 18.3 collective-permute-start
  99.7 14.9 collective-permute-start.1
  132.2 27.5 %all-to-all-start = ((f32[1,6,640,80]{3,0,1,2:T(1,128)}), f32[1,6,640,80]{3,0,1,2:T(1,128)S(1)}, u32[]{:S(2)}, u32[]{:S(2)}) async-start(f32[1,6,640,80]{3,0,1,2:T(1,128)} %copy.143), calls=%async_computation | async-start | bytes 3932160 | tf_op jit(solution)/shard_map/while/body/eval_jaxpr/all_to_all | solution.py:106
  280.0 17.9 collective-permute-start
  283.2 16.2 collective-permute-start.1
  317.1 27.5 %all-to-all-start = ((f32[1,6,640,80]{3,0,1,2:T(1,128)}), f32[1,6,640,80]{3,0,1,2:T(1,128)S(1)}, u32[]{:S(2)}, u32[]{:S(2)}) async-start(f32[1,6,640,80]{3,0,1,2:T(1,128)} %copy.143), calls=%async_computation | async-start | bytes 3932160 | tf_op jit(solution)/shard_map/while/body/eval_jaxpr/all_to_all | solution.py:106
  464.2 18.2 collective-permute-start
  466.6 15.7 collective-permute-start.1
  500.0 28.5 %all-to-all-start = ((f32[1,6,640,80]{3,0,1,2:T(1,128)}), f32[1,6,640,80]{3,0,1,2:T(1,128)S(1)}, u32[]{:S(2)}, u32[]{:S(2)}) async-start(f32[1,6,640,80]{3,0,1,2:T(1,128)} %copy.143), calls=%async_computation | async-start | bytes 3932160 | tf_op jit(solution)/shard_map/while/body/eval_jaxpr/all_to_all | solution.py:106
  649.1 17.7 collective-permute-start
  651.5 15.5 collective-permute-start.1
  684.6 28.8 %all-to-all-start = ((f32[1,6,640,80]{3,0,1,2:T(1,128)}), f32[1,6,640,80]{3,0,1,2:T(1,128)S(1)}, u32[]{:S(2)}, u32[]{:S(2)}) async-start(f32[1,6,640,80]{3,0,1,2:T(1,128)} %copy.143), calls=%async_computation | async-start | bytes 3932160 | tf_op jit(solution)/shard_map/while/body/eval_jaxpr/all_to_all | solution.py:106
  832.4 17.8 collective-permute-start
  834.9 15.4 collective-permute-start.1
  868.0 28.8 %all-to-all-start = ((f32[1,6,640,80]{3,0,1,2:T(1,128)}), f32[1,6,640,80]{3,0,1,2:T(1,128)S(1)}, u32[]{:S(2)}, u32[]{:S(2)}) async-start(f32[1,6,640,80]{3,0,1,2:T(1,128)} %copy.143), calls=%async_computation | async-start | bytes 3932160 | tf_op jit(solution)/shard_map/while/body/eval_jaxpr/all_to_all | solution.py:106
  1017.3 17.9 collective-permute-start
  1020.5 16.2 collective-permute-start.1
  1054.4 27.5 %all-to-all-start = ((f32[1,6,640,80]{3,0,1,2:T(1,128)}), f32[1,6,640,80]{3,0,1,2:T(1,128)S(1)}, u32[]{:S(2)}, u32[]{:S(2)}) async-start(f32[1,6,640,80]{3,0,1,2:T(1,128)} %copy.143), calls=%async_computation | async-start | bytes 3932160 | tf_op jit(solution)/shard_map/while/body/eval_jaxpr/all_to_all | solution.py:106
  1201.1 17.8 collective-permute-start
  1203.5 15.5 collective-permute-start.1
  1236.7 28.7 %all-to-all-start = ((f32[1,6,640,80]{3,0,1,2:T(1,128)}), f32[1,6,640,80]{3,0,1,2:T(1,128)S(1)}, u32[]{:S(2)}, u32[]{:S(2)}) async-start(f32[1,6,640,80]{3,0,1,2:T(1,128)} %copy.143), calls=%async_computation | async-start | bytes 3932160 | tf_op jit(solution)/shard_map/while/body/eval_jaxpr/all_to_all | solution.py:106
  1386.4 17.7 collective-permute-start
  1388.8 15.5 collective-permute-start.1
  1421.9 28.8 %all-to-all-start = ((f32[1,6,640,80]{3,0,1,2:T(1,128)}), f32[1,6,640,80]{3,0,1,2:T(1,128)S(1)}, u32[]{:S(2)}, u32[]{:S(2)}) async-start(f32[1,6,640,80]{3,0,1,2:T(1,128)} %copy.143), calls=%async_computation | async-start | bytes 3932160 | tf_op jit(solution)/shard_map/while/body/eval_jaxpr/all_to_all | solution.py:106
  1570.2 17.8 collective-permute-start
  1572.6 15.4 collective-permute-start.1
  1605.7 28.8 %all-to-all-start = ((f32[1,6,640,80]{3,0,1,2:T(1,128)}), f32[1,6,640,80]{3,0,1,2:T(1,128)S(1)}, u32[]{:S(2)}, u32[]{:S(2)}) async-start(f32[1,6,640,80]{3,0,1,2:T(1,128)} %copy.143), calls=%async_computation | async-start | bytes 3932160 | tf_op jit(solution)/shard_map/while/body/eval_jaxpr/all_to_all | solution.py:106
  1754.6 18.3 collective-permute-start
  1757.1 15.8 collective-permute-start.1
  1790.6 28.5 %all-to-all-start = ((f32[1,6,640,80]{3,0,1,2:T(1,128)}), f32[1,6,640,80]{3,0,1,2:T(1,128)S(1)}, u32[]{:S(2)}, u32[]{:S(2)}) async-start(f32[1,6,640,80]{3,0,1,2:T(1,128)} %copy.143), calls=%async_computation | async-start | bytes 3932160 | tf_op jit(solution)/shard_map/while/body/eval_jaxpr/all_to_all | solution.py:106
where the time goes:
time: 1930 us; the launch traced here: 1920 us
  local copies, waits for them, and re-layouts  729 us (38%)
  waiting for transfers between devices  390 us (20%)
  blocking collectives  389 us (20%)
  matrix products  200 us (10%)
  other arithmetic  112 us (6%)
  starting transfers between devices  76.9 us (4%)
  loops' own time  22.6 us (1%)
    psum x10, blocking collectives, advance(): command = lax.psum(partial_cmd, ('layer', 'sub'))  389 us
    all_to_all x10, waiting for transfers between devices, advance(): lax.all_to_all(window, 'layer', split_axis=2, concat_axis=0, tiled=True)  234 us
    sin x50, local copies, waits for them, and re-layouts, lenslet_slopes(): imag_part = jnp.sin(tiles)  183 us
    cos x40, local copies, waits for them, and re-layouts, lenslet_slopes(): real_part = jnp.cos(tiles)  166 us
    ppermute x10, waiting for transfers between devices, extended_2(): lax.ppermute(lax.slice_in_dim(block, 0, width, axis=dim), axis, backward)  151 us
    gather x180, local copies, waits for them, and re-layouts  128 us
    dot_general x10, matrix products, advance(): partial_cmd = jnp.dot(flat, matrix, preferred_element_type=jnp.float32)  103 us
    select_n x10, local copies, waits for them, and re-layouts, place_columns(): return jnp.where(inside, placed, strips)  72.3 us
  transfers between devices with their start and end apart: 30, of which 26 were waited for; matrix products, arithmetic and copies ran while one was open for 0% of the time, Pallas kernels for 0%

commit v1 on v0

v1 whole, which is shorter than its diff:
```python
import functools
import math

import jax
import jax.numpy as jnp
import numpy as np
from jax import lax
from jax.experimental import pallas as pl
from jax.experimental.pallas import tpu as pltpu
from jax.sharding import PartitionSpec as P

FFT_LEN = 16
ACTS = 5376
HALO = 40
NEW_COLS = 8
PUP = 640
PUP_TURN = 3
ROW0 = 704
PIX = 8
LANES = 128
GROUP = 3
SUBS = 16


def sin_cos(x):
    k = jnp.floor(x * np.float32(2.0 / math.pi) + np.float32(0.5))
    r = x - k * np.float32(1.5703125)
    r = r - k * np.float32(4.837512969970703125e-4)
    r = r - k * np.float32(7.54978995489188216e-8)
    z = r * r
    sr = (np.float32(-1.9515295891e-4) * z + np.float32(8.3321608736e-3)) * z
    sr = r + r * z * (sr + np.float32(-1.6666654611e-1))
    cr = (np.float32(2.443315711809948e-5) * z + np.float32(-1.388731625493765e-3)) * z
    cr = z * z * (cr + np.float32(4.166664568298827e-2))
    cr = cr - np.float32(0.5) * z + np.float32(1.0)
    q = k.astype(jnp.int32)
    swap = (q & 1) == 1
    s = jnp.where(swap, cr, sr)
    c = jnp.where(swap, sr, cr)
    s = jnp.where((q & 2) == 2, -s, s)
    c = jnp.where(((q + 1) & 2) == 2, -c, c)
    return s, c


def split(x):
    high = x.astype(jnp.bfloat16)
    low = (x - high.astype(jnp.float32)).astype(jnp.bfloat16)
    return high, low


def lenslet_constants(cols, used):
    place = np.arange(PIX)
    diff = place[:, None] - place[None, :]
    gap = np.where(diff == 0, 1, np.abs(diff))
    weight = -((-1.0) ** gap) / np.tan(np.pi * gap / FFT_LEN)
    odd = np.where(diff == 0, 0.0, np.sign(diff) * weight)
    sign = (-1.0) ** place
    even = -0.5 * sign[:, None] * sign[None, :]

    def parts(mat):
        high = mat.astype(jnp.bfloat16)
        return high, (mat - high.astype(np.float64)).astype(jnp.bfloat16)

    odd_c = np.kron(np.eye(cols // PIX), odd)
    even_c = np.kron(np.eye(cols // PIX), even).astype(jnp.bfloat16)
    high, low = parts(odd_c)
    zero = np.zeros_like(high)
    left_c = np.concatenate(
        [np.concatenate([high, high, low], 1), np.concatenate([even_c, even_c, zero], 1)], 0
    )
    left_s = np.concatenate([even_c, even_c], 1)
    high, low = parts(np.kron(np.eye(LANES // PIX), odd.T))
    even_r = np.kron(np.eye(LANES // PIX), even).astype(jnp.bfloat16)
    zero = np.zeros_like(high)
    right_c = np.concatenate(
        [np.concatenate([high, low], 1), np.concatenate([high, zero], 1)], 0
    )
    right_e = np.concatenate([even_r, even_r], 0)
    sum_l = np.zeros((SUBS, cols))
    for c in range(used):
        sum_l[c // PIX, c] = 1.0
    sum_l = np.concatenate([sum_l, sum_l], 1).astype(jnp.bfloat16)
    sum_r = np.zeros((LANES, LANES))
    for c in range(LANES):
        sum_r[c, c // PIX] = 1.0
    sum_r = np.concatenate([sum_r, sum_r], 0).astype(jnp.bfloat16)
    return [jnp.asarray(m) for m in (left_c, left_s, right_c, right_e, sum_l, sum_r)]


def mm(a, b):
    return jnp.dot(a, b, preferred_element_type=jnp.float32)


def lenslet_kernel(
    layers, stars, rows, cols, ext,
    blk_ref, sx_ref, sy_ref, band_ref,
    left_c_ref, left_s_ref, right_c_ref, right_e_ref, sum_l_ref, sum_r_ref,
    out_ref, screen_ref,
):
    main = rows // LANES
    rem = rows % LANES
    tiles = band_ref.shape[2] // LANES
    groups = stars // GROUP
    lane = lax.broadcasted_iota(jnp.int32, (cols, LANES), 1)

    for l in range(layers):
        for j in range(tiles):
            screen_ref[l, j, 0:ext, :] = band_ref[l, 0:ext, j * LANES : (j + 1) * LANES]

    def body(i, carry):
        t = i // groups
        h = i % groups
        for l in range(layers):
            start = pl.multiple_of(blk_ref[t * layers + l] * NEW_COLS, NEW_COLS)
            row = pl.multiple_of(ext + t * NEW_COLS, NEW_COLS)
            for j in range(tiles):
                screen_ref[l, j, pl.ds(start, NEW_COLS), :] = band_ref[
                    l, pl.ds(row, NEW_COLS), j * LANES : (j + 1) * LANES
                ]
        parts = []
        tail = None
        for k in range(GROUP):
            sums = [None] * (main + 1)
            for l in range(layers):
                at = (t * layers + l) * stars + h * GROUP + k
                dx = sx_ref[at] + HALO
                dy = sy_ref[at] + HALO
                turn = lax.rem(LANES - dy, LANES)
                rolled = [
                    pltpu.roll(screen_ref[l, j, pl.ds(dx, cols), :], turn, 1)
                    for j in range(main + 1)
                ]
                keep = lane < LANES - dy
                for j in range(main + 1):
                    if j < main:
                        piece = jnp.where(keep, rolled[j], rolled[j + 1])
                    else:
                        piece = rolled[j]
                    sums[j] = piece if sums[j] is None else sums[j] + piece
            parts.extend(sums[:main])
            if rem:
                moved = sums[main] if k == 0 else pltpu.roll(sums[main], k * rem, 1)
                tail = moved if tail is None else jnp.where(lane < k * rem, tail, moved)
        if rem:
            parts.append(tail)
        phase = jnp.concatenate(parts, axis=1)
        s, c = sin_cos(phase)
        ch, cl = split(c)
        sh, sl = split(s)
        from_c = mm(left_c_ref[...], jnp.concatenate([ch, cl, ch], axis=0))
        from_s = mm(left_s_ref[...], jnp.concatenate([sh, sl], axis=0))
        along_x = s * (from_c[0:cols] + from_s) + c * from_c[cols:]
        power = c * c + s * s
        along_y = []
        for j in range(len(parts)):
            cut = slice(j * LANES, (j + 1) * LANES)
            pair_c = jnp.concatenate([ch[:, cut], cl[:, cut]], axis=1)
            pair_s = jnp.concatenate([sh[:, cut], sl[:, cut]], axis=1)
            odd = mm(pair_c, right_c_ref[...])
            odd = odd[:, :LANES] + odd[:, LANES:]
            along_y.append(
                s[:, cut] * (odd + mm(pair_s, right_e_ref[...]))
                + c[:, cut] * mm(pair_c, right_e_ref[...])
            )
        every = jnp.concatenate([along_x] + along_y + [power], axis=1)
        high, low = split(every)
        every = mm(sum_l_ref[...], jnp.concatenate([high, low], axis=0))
        count = 3 * len(parts)
        every = jnp.concatenate(
            [every[:, j * LANES : (j + 1) * LANES] for j in range(count)], axis=0
        )
        high, low = split(every)
        every = mm(jnp.concatenate([high, low], axis=1), sum_r_ref[...])
        size = len(parts) * SUBS
        total = every[2 * size :]
        out_ref[i, 0] = every[:size] / total
        out_ref[i, 1] = every[size : 2 * size] / total
        return carry

    lax.fori_loop(0, blk_ref.shape[0] // layers * groups, body, 0)


def lenslet_slopes(band, blocks, step_x, step_y, rows, cols, ext, interpret=False):
    steps, layers, stars = step_x.shape
    padded = ext - 2 * HALO
    main = rows // LANES
    tiles = GROUP * main + (1 if rows % LANES else 0)
    groups = stars // GROUP
    smem = pl.BlockSpec(memory_space=pltpu.SMEM)
    vmem = pl.BlockSpec(memory_space=pltpu.VMEM)
    out = pl.pallas_call(
        functools.partial(lenslet_kernel, layers, stars, rows, padded, ext),
        out_shape=jax.ShapeDtypeStruct((steps * groups, 2, tiles * SUBS, LANES), jnp.float32),
        in_specs=[smem] * 3 + [vmem] * 7,
        out_specs=vmem,
        scratch_shapes=[
            pltpu.VMEM((layers, band.shape[2] // LANES, ext + NEW_COLS, LANES), jnp.float32)
        ],
        compiler_params=pltpu.CompilerParams(vmem_limit_bytes=40 * 1024 * 1024),
        interpret=interpret,
    )(
        blocks.reshape(-1), step_x.reshape(-1), step_y.reshape(-1), band,
        *lenslet_constants(padded, cols),
    )
    out = out.reshape(steps, groups, 2, tiles, SUBS, LANES)[:, :, :, :, : cols // PIX]
    found = []
    if main:
        part = out[:, :, :, : GROUP * main, :, : LANES // PIX]
        part = part.reshape(steps, groups, 2, GROUP, main, cols // PIX, LANES // PIX)
        part = jnp.transpose(part, (0, 1, 3, 5, 2, 4, 6))
        found.append(part.reshape(steps, stars, cols // PIX, 2, main * LANES // PIX))
    rem = rows % LANES // PIX
    if rem:
        part = out[:, :, :, GROUP * main, :, : GROUP * rem]
        part = part.reshape(steps, groups, 2, cols // PIX, GROUP, rem)
        part = jnp.transpose(part, (0, 1, 4, 3, 2, 5))
        found.append(part.reshape(steps, stars, cols // PIX, 2, rem))
    return jnp.concatenate(found, axis=4) if len(found) > 1 else found[0]


def local(screens, new_columns, col_block, shift_x, shift_y, valid, recon):
    width = screens.shape[3]
    steps, _, stars = shift_x.shape
    count = lax.axis_size("layer")
    owner = lax.axis_index("sub")
    subs = lax.axis_size("sub")
    rows = valid.shape[0] * PIX
    cols = -(-width // 16) * 16
    ext = cols + 2 * HALO
    lanes = -(-(rows + 2 * HALO) // LANES) * LANES

    band = screens[0, PUP_TURN - 1 : PUP_TURN + 2, ROW0 - HALO : ROW0 + PUP + HALO, :]
    band = jnp.transpose(band, (0, 2, 1))
    tail = jnp.where(owner == subs - 1, band[0, width - HALO :], band[1, width - HALO :])
    head = jnp.where(owner == 0, band[2, :HALO], band[1, :HALO])
    forward = [(i, (i + 1) % subs) for i in range(subs)]
    backward = [(b, a) for a, b in forward]
    before = lax.ppermute(tail, "sub", forward)
    after = lax.ppermute(head, "sub", backward)
    fresh = jnp.transpose(new_columns[:, 0, ROW0 - HALO : ROW0 + PUP + HALO, :], (0, 2, 1))
    fresh = fresh.reshape(steps * NEW_COLS, PUP + 2 * HALO)
    pieces = [before, band[1], after]
    if cols > width:
        pieces.append(jnp.zeros((cols - width, PUP + 2 * HALO), jnp.float32))
    strip = jnp.concatenate(pieces + [fresh], axis=0)
    plan = jnp.concatenate(
        [col_block.reshape(-1), shift_x.reshape(-1), shift_y.reshape(-1)]
    ).astype(jnp.float32)
    lines = -(-plan.shape[0] // lanes)
    plan = jnp.pad(plan, (0, 8 * lanes - plan.shape[0])).reshape(8, lanes)

    def share(i):
        cut = strip[:, i * rows : i * rows + rows + 2 * HALO]
        cut = jnp.pad(cut, ((0, 0), (0, lanes - cut.shape[1])))
        return jnp.concatenate([cut, plan], axis=0)

    sent = jnp.stack([share(i) for i in range(count)])
    got = lax.all_to_all(sent, "layer", split_axis=0, concat_axis=0, tiled=True)

    last = ext + steps * NEW_COLS
    plans = got[:, last : last + lines].reshape(count, -1).astype(jnp.int32)
    blocks = plans[:, :steps].T
    step_x = plans[:, steps : steps + steps * stars].reshape(count, steps, stars)
    step_y = plans[:, steps + steps * stars : steps + 2 * steps * stars]
    step_x = jnp.transpose(step_x, (1, 0, 2))
    step_y = jnp.transpose(step_y.reshape(count, steps, stars), (1, 0, 2))
    spot = blocks - PUP_TURN * PUP // NEW_COLS - owner * (width // NEW_COLS) + HALO // NEW_COLS
    inside = (spot >= 0) & (spot < (width + 2 * HALO) // NEW_COLS)
    spot = jnp.where(inside, spot, ext // NEW_COLS)

    slopes = lenslet_slopes(got, spot, step_x, step_y, rows, width, ext)
    slopes = slopes * valid.T.astype(jnp.float32)[None, None, :, None, :]
    flat = jnp.transpose(slopes, (0, 1, 4, 2, 3)).astype(jnp.bfloat16).reshape(steps, -1)
    matrix = jnp.transpose(recon, (0, 2, 3, 1, 4)).reshape(-1, ACTS)
    part = jnp.dot(flat, matrix, preferred_element_type=jnp.float32)
    commands = lax.psum(part, ("layer", "sub"))
    return (jnp.transpose(slopes, (0, 1, 3, 4, 2)), commands)


def solution(mesh):
    return jax.shard_map(
        local,
        mesh=mesh,
        in_specs=(
            P("layer", None, None, "sub"),
            P(None, "layer", None, None),
            P(None, "layer"),
            P(None, "layer", None),
            P(None, "layer", None),
            P("layer", "sub"),
            P(None, None, "layer", "sub", None),
        ),
        out_specs=(P(None, None, None, "layer", "sub"), P()),
        check_vma=False,
    )
```

time: 1930 us -> 220 us (0.11)
  local copies, waits for them, and re-layouts: 729 us -> 13.6 us
  blocking collectives: 389 us -> 0 us
  waiting for transfers between devices: 390 us -> 139 us
  matrix products: 200 us -> 14.2 us
  other arithmetic: 112 us -> 4.9 us
  starting transfers between devices: 76.9 us -> 10.5 us
  Pallas kernels: 0 us -> 23 us
  loops' own time: 22.6 us -> 0 us
    psum x10 -> x0, blocking collectives: 389 us -> none  [advance(): command = lax.psum(partial_cmd, ('layer', 'sub'))]
    all_to_all x10 -> x1, waiting for transfers between devices: 234 us -> 12.5 us  [local(): got = lax.all_to_all(sent, 'layer', split_axis=0, concat_axis=0, tiled=True)]
    dot_general x90 -> x1, matrix products: 200 us -> 14.2 us  [local(): part = jnp.dot(flat, matrix, preferred_element_type=jnp.float32)]
    sin x50 -> x0, local copies, waits for them, and re-layouts: 183 us -> none  [lenslet_slopes(): imag_part = jnp.sin(tiles)]
    cos x40 -> x0, local copies, waits for them, and re-layouts: 166 us -> none  [lenslet_slopes(): real_part = jnp.cos(tiles)]
    gather x200 -> x0, local copies, waits for them, and re-layouts: 162 us -> none
    ppermute x20 -> x2, waiting for transfers between devices: 156 us -> 0.01 us  [the longest x1 0.01 us: local(): after = lax.ppermute(head, 'sub', backward)]
    psum x0 -> x1, waiting for transfers between devices: none -> 126 us  [local(): commands = lax.psum(part, ('layer', 'sub'))]
  transfers between devices with their start and end apart: 30 -> 4, of which waited for: 26 -> 2; matrix products, arithmetic and copies ran while one was open for 0% -> 2% of each run, Pallas kernels for 0% -> 0%
where the time goes in v1:
time: 220 us; the launch traced here: 219 us
  waiting for transfers between devices  139 us (63%)
  Pallas kernels  23 us (10%)
  matrix products  14.2 us (6%)
  between operations  14.2 us (6%)
  local copies, waits for them, and re-layouts  13.6 us (6%)
  starting transfers between devices  10.5 us (5%)
  other arithmetic  4.9 us (2%)
    psum x1, waiting for transfers between devices, local(): commands = lax.psum(part, ('layer', 'sub'))  126 us
    pallas_call x1, Pallas kernels, lenslet_slopes(): pl.pallas_call(functools.partial(lenslet_kernel, layers, stars, rows, pad...  23 us
    dot_general x1, matrix products, local(): part = jnp.dot(flat, matrix, preferred_element_type=jnp.float32)  14.2 us
    all_to_all x1, waiting for transfers between devices, local(): got = lax.all_to_all(sent, 'layer', split_axis=0, concat_axis=0, tiled=True)  12.5 us
    unnamed x17, local copies, waits for them, and re-layouts  8.61 us
    all_to_all x1, starting transfers between devices, local(): got = lax.all_to_all(sent, 'layer', split_axis=0, concat_axis=0, tiled=True)  5.25 us
  transfers between devices with their start and end apart: 4, of which 2 were waited for; matrix products, arithmetic and copies ran while one was open for 2% of the time, Pallas kernels for 0%

profile of v1, /device:TPU:1, one launch (start us, length us, event | category | flops | bytes accessed | tf_op | source)
XLA Modules:
  0.0 219.2 jit_solution(9254826388579640041)
XLA Ops:
  7.2 1.4 slice_bitcast_fusion.1
  8.6 2.1 collective-permute-start
  10.7 3.1 %collective-permute-start.1 = (f32[40,720]{1,0:T(8,128)S(1)}, f32[40,720]{1,0:T(8,128)S(1)}, u32[]{:S(2)}, u32[]{:S(2)}) collective-permute-start(f32[40,720]{1,0:T(8,128)S(1)} %get-tuple-element.8), channel_id=1, source_target_pairs={{1,0},{2,1},{3,2},{4,3},{5,4},{6,5},{7,6},{0,7},{9,8},{10,9},{11,1... | collective-permute-start | bytes 345608 | tf_op jit(solution)/shard_map/ppermute | solution.py:239
  13.9 1.1 slice_bitcast_fusion.3
  15.0 0.8 copy.22
  15.7 0.1 reshape.57
  15.8 0.8 copy.23
  16.6 0.1 reshape.58
  16.7 0.7 add_convert_fusion
  17.4 0.0 collective-permute-done
  17.4 0.0 collective-permute-done.1
  17.4 0.1 pad_maximum_fusion.1
  17.5 0.3 fusion.16
  17.8 0.7 slice_select_fusion
  18.4 0.1 fusion.6
  18.5 1.0 pad_maximum_fusion
  19.6 5.2 %all-to-all-start = ((f32[4,248,256]{2,1,0:T(8,128)}), f32[4,248,256]{2,1,0:T(8,128)S(1)}, u32[]{:S(2)}, u32[]{:S(2)}) async-start(f32[4,248,256]{2,1,0:T(8,128)} %pad_maximum_fusion), calls=%async_computation | async-start | bytes 2031616 | tf_op jit(solution)/shard_map/all_to_all | solution.py:258
  24.8 0.0 all-reduce.6.cloned.1.call-start
  24.8 0.7 convert_bitcast_fusion.1
  25.5 12.5 %all-to-all-done.band_ref = f32[4,248,256]{2,1,0:T(8,128)S(1)} async-done(((f32[4,248,256]{2,1,0:T(8,128)}), f32[4,248,256]{2,1,0:T(8,128)S(1)}, u32[]{:S(2)}, u32[]{:S(2)}) %all-to-all-start) | async-done | bytes 1015840 | tf_op jit(solution)/shard_map/all_to_all | solution.py:258
  38.1 0.1 fusion.17
  38.1 0.1 copy.24
  38.2 0.1 reshape.60.blk_ref
  38.3 0.1 reshape.63
  38.4 0.1 reshape.64.sy_ref
  38.5 0.1 reshape.61
  38.7 0.1 reshape.62.sx_ref
  38.8 0.0 copy-start
  38.8 0.9 copy-done
  39.7 0.0 copy-start.1
  39.7 0.9 copy-done.1
  40.6 0.0 copy-start.2
  40.6 0.8 copy-done.2
  41.4 0.0 copy-start.3
  41.4 0.8 copy-done.3
  42.2 0.0 copy-start.4
  42.2 0.8 copy-done.4
  43.0 0.0 copy-start.5
  43.0 0.7 copy-done.5
  43.7 23.0 %shard_map.140 = f32[20,2,64,128]{3,2,1,0:T(8,128)S(1)} custom-call(s32[40]{0:T(128)S(1)} %reshape.60.blk_ref, s32[240]{0:T(256)S(1)} %reshape.62.sx_ref, s32[240]{0:T(256)S(1)} %reshape.64.sy_ref, f32[4,248,256]{2,1,0:T(8,128)S(1)} %all-to-all-done.band_ref, bf16[160,240]{1,0:T(8,128)(2,1)S(1)} %copy-done.1, bf16[80,160]{1,0:T(8,128)(2,1)S(1)} %copy-done.4, ...), custom_call_target="tpu_custom_call" | custom-call | tf_op jit(solution)/shard_map/pallas_call | solution.py:191
  66.8 0.1 slice_bitcast_fusion
  66.9 0.3 copy.27
  67.2 0.4 copy.34
  67.6 1.0 copy.29
  68.6 1.6 convert_bitcast_fusion
  70.1 14.2 %fusion.2 = f32[10,5376]{1,0:T(8,128)} fusion(bf16[6,20,10,2,5376]{4,3,2,1,0:T(2,128)(2,1)} %bitcast.69, bf16[10,6,20,10,2]{2,4,3,1,0:T(2,128)(2,1)S(1)} %get-tuple-element.2), kind=kOutput, calls=%fused_computation.2 | convolution fusion | flops 258048000 | bytes 26067840 | tf_op jit(solution)/shard_map/dot_general | solution.py:275
  84.4 0.0 all-reduce.6.cloned.1.call-update
  84.4 126.3 %all-reduce.6.cloned.1.call-done = f32[10,5376]{1,0:T(8,128)} async-done(((f32[10,5376]{1,0:T(8,128)}), f32[10,5376]{1,0:T(8,128)}) %all-reduce.6.cloned.1.call-update) | async-done | bytes 215056 | tf_op jit(solution)/shard_map/psum | solution.py:276
  210.6 1.7 copy.44
  (10 shorter events, 0.1 us)
Async XLA Ops:
  8.6 8.8 %collective-permute-start = (f32[40,720]{1,0:T(8,128)S(1)}, f32[40,720]{1,0:T(8,128)S(1)}, u32[]{:S(2)}, u32[]{:S(2)}) collective-permute-start(f32[40,720]{1,0:T(8,128)S(1)} %get-tuple-element.7), channel_id=1, source_target_pairs={{0,1},{1,2},{2,3},{3,4},{4,5},{5,6},{6,7},{7,0},{8,9},{9,10},{10,1... | collective-permute-start | bytes 345608 | tf_op jit(solution)/shard_map/ppermute | solution.py:238
  10.7 6.7 %collective-permute-start.1 = (f32[40,720]{1,0:T(8,128)S(1)}, f32[40,720]{1,0:T(8,128)S(1)}, u32[]{:S(2)}, u32[]{:S(2)}) collective-permute-start(f32[40,720]{1,0:T(8,128)S(1)} %get-tuple-element.8), channel_id=1, source_target_pairs={{1,0},{2,1},{3,2},{4,3},{5,4},{6,5},{7,6},{0,7},{9,8},{10,9},{11,1... | collective-permute-start | bytes 345608 | tf_op jit(solution)/shard_map/ppermute | solution.py:239
  19.6 18.5 %all-to-all-start = ((f32[4,248,256]{2,1,0:T(8,128)}), f32[4,248,256]{2,1,0:T(8,128)S(1)}, u32[]{:S(2)}, u32[]{:S(2)}) async-start(f32[4,248,256]{2,1,0:T(8,128)} %pad_maximum_fusion), calls=%async_computation | async-start | bytes 2031616 | tf_op jit(solution)/shard_map/all_to_all | solution.py:258
  24.8 185.8 %all-reduce.6.cloned.1.call-start = ((), (), s32[]{:S(2)}) async-start(), calls=%async_computation.1 | async-start | bytes 688128 | tf_op jit(solution)/shard_map/psum | solution.py:276
  38.8 0.9 copy-start
  39.7 0.9 copy-start.1
  40.6 0.8 copy-start.2
  41.4 0.8 copy-start.3
  42.2 0.8 copy-start.4
  43.0 0.7 copy-start.5
Sparse Core Ops, SparseCore 0:
  84.5 126.0 all-reduce.5

commit v2 on v1

--- a/solution.py
+++ b/solution.py
@@ -218,6 +218,98 @@
     return jnp.concatenate(found, axis=4) if len(found) > 1 else found[0]
 
 
+def sum_kernel(
+    part_ref, out_ref, by_layer, by_sub, mine,
+    send_1, recv_1, send_2, recv_2, send_3, recv_3, send_4, recv_4,
+):
+    layers, subs = part_ref.shape[0], part_ref.shape[1]
+    me_l = lax.axis_index("layer")
+    me_s = lax.axis_index("sub")
+    mesh_id = pl.DeviceIdType.MESH
+    layer_peers = [lax.rem(me_l + j, layers) for j in range(1, layers)]
+    sub_peers = [lax.rem(me_s + j, subs) for j in range(1, subs)]
+
+    barrier = pltpu.get_barrier_semaphore()
+    for p in layer_peers:
+        pl.semaphore_signal(barrier, inc=1, device_id=(p, me_s), device_id_type=mesh_id)
+    for q in sub_peers:
+        pl.semaphore_signal(barrier, inc=1, device_id=(me_l, q), device_id_type=mesh_id)
+    pl.semaphore_wait(barrier, layers + subs - 2)
+
+    def push(src, dst, send, recv, j, target):
+        copy = pltpu.make_async_remote_copy(
+            src_ref=src, dst_ref=dst, send_sem=send.at[j], recv_sem=recv.at[j],
+            device_id=target, device_id_type=mesh_id,
+        )
+        copy.start()
+        return copy
+
+    copies = [
+        push(part_ref.at[p], by_layer.at[j], send_1, recv_1, j, (p, me_s))
+        for j, p in enumerate(layer_peers)
+    ]
+    for copy in copies:
+        copy.wait()
+    total = part_ref[me_l]
+    for j in range(layers - 1):
+        total = total + by_layer[j]
+    mine[...] = total
+
+    copies = [
+        push(mine.at[q], by_sub.at[j], send_2, recv_2, j, (me_l, q))
+        for j, q in enumerate(sub_peers)
+    ]
+    for copy in copies:
+        copy.wait()
+    total = mine[me_s]
+    for j in range(subs - 1):
+        total = total + by_sub[j]
+    out_ref[me_l, me_s] = total
+
+    own = out_ref.at[me_l, me_s]
+    copies = [
+        push(own, own, send_3, recv_3, j, (me_l, q)) for j, q in enumerate(sub_peers)
+    ]
+    for copy in copies:
+        copy.wait()
+    own = out_ref.at[me_l]
+    copies = [
+        push(own, own, send_4, recv_4, j, (p, me_s)) for j, p in enumerate(layer_peers)
+    ]
+    for copy in copies:
+        copy.wait()
+
+
+def summed_everywhere(part):
+    layers = lax.axis_size("layer")
+    subs = lax.axis_size("sub")
+    lines = part.size // LANES
+    chunk = -(-lines // (layers * subs * 8)) * 8
+    padded = jnp.pad(part.reshape(lines, LANES), ((0, layers * subs * chunk - lines), (0, 0)))
+    padded = padded.reshape(layers, subs, chunk, LANES)
+    vmem = pl.BlockSpec(memory_space=pltpu.VMEM)
+    dma = pltpu.SemaphoreType.DMA
+    total = pl.pallas_call(
+        sum_kernel,
+        out_shape=jax.ShapeDtypeStruct(padded.shape, jnp.float32),
+        in_specs=[vmem],
+        out_specs=vmem,
+        scratch_shapes=[
+            pltpu.VMEM((layers - 1, subs, chunk, LANES), jnp.float32),
+            pltpu.VMEM((subs - 1, chunk, LANES), jnp.float32),
+            pltpu.VMEM((subs, chunk, LANES), jnp.float32),
+            dma((layers - 1,)), dma((layers - 1,)),
+            dma((subs - 1,)), dma((subs - 1,)),
+            dma((subs - 1,)), dma((subs - 1,)),
+            dma((layers - 1,)), dma((layers - 1,)),
+        ],
+        compiler_params=pltpu.CompilerParams(
+            collective_id=0, has_side_effects=True, vmem_limit_bytes=32 * 1024 * 1024
+        ),
+    )(padded)
+    return total.reshape(-1, LANES)[:lines].reshape(part.shape)
+
+
 def local(screens, new_columns, col_block, shift_x, shift_y, valid, recon):
     width = screens.shape[3]
     steps, _, stars = shift_x.shape
@@ -273,7 +365,7 @@
     flat = jnp.transpose(slopes, (0, 1, 4, 2, 3)).astype(jnp.bfloat16).reshape(steps, -1)
     matrix = jnp.transpose(recon, (0, 2, 3, 1, 4)).reshape(-1, ACTS)
     part = jnp.dot(flat, matrix, preferred_element_type=jnp.float32)
-    commands = lax.psum(part, ("layer", "sub"))
+    commands = summed_everywhere(part)
     return (jnp.transpose(slopes, (0, 1, 3, 4, 2)), commands)
 
 

time: 220 us -> 98.8 us (0.45)
  waiting for transfers between devices: 139 us -> 12.6 us
  Pallas kernels: 23 us -> 43.1 us
  between operations: 14.2 us -> 0.8 us
    psum x1 -> x0, waiting for transfers between devices: 126 us -> none  [local(): commands = lax.psum(part, ('layer', 'sub'))]
    pallas_call x0 -> x1, Pallas kernels: none -> 20.1 us  [summed_everywhere(): pl.pallas_call(sum_kernel, out_shape=jax.ShapeDtypeStruct(padded.shape, j...]
    unnamed x17 -> x16, local copies, waits for them, and re-layouts: 8.61 us -> 6.86 us
  transfers between devices with their start and end apart: 4 -> 3, of which waited for: 2 -> 1; matrix products, arithmetic and copies ran while one was open for 2% -> 4% of each run, Pallas kernels for 0% -> 0%
where the time goes in v2:
time: 98.8 us; the launch traced here: 98.1 us
  Pallas kernels  43.1 us (44%)
  matrix products  13.6 us (14%)
  local copies, waits for them, and re-layouts  12.7 us (13%)
  waiting for transfers between devices  12.6 us (13%)
  starting transfers between devices  10.5 us (11%)
  other arithmetic  4.9 us (5%)
    pallas_call x1, Pallas kernels, lenslet_slopes(): pl.pallas_call(functools.partial(lenslet_kernel, layers, stars, rows, pad...  23 us
    pallas_call x1, Pallas kernels, summed_everywhere(): pl.pallas_call(sum_kernel, out_shape=jax.ShapeDtypeStruct(padded.shape, j...  20.1 us
    dot_general x1, matrix products, local(): part = jnp.dot(flat, matrix, preferred_element_type=jnp.float32)  13.6 us
    all_to_all x1, waiting for transfers between devices, local(): got = lax.all_to_all(sent, 'layer', split_axis=0, concat_axis=0, tiled=True)  12.5 us
    unnamed x16, local copies, waits for them, and re-layouts  6.86 us
    all_to_all x1, starting transfers between devices, local(): got = lax.all_to_all(sent, 'layer', split_axis=0, concat_axis=0, tiled=True)  5.25 us
    ppermute x1, starting transfers between devices, local(): after = lax.ppermute(head, 'sub', backward)  3.1 us
    ppermute x1, starting transfers between devices, local(): before = lax.ppermute(tail, 'sub', forward)  2.12 us
  transfers between devices with their start and end apart: 3, of which 1 were waited for; matrix products, arithmetic and copies ran while one was open for 4% of the time, Pallas kernels for 0%

profile of v2, /device:TPU:1, one launch (start us, length us, event | category | flops | bytes accessed | tf_op | source)
XLA Modules:
  0.0 98.1 jit_solution(2115949647856266910)
XLA Ops:
  0.6 1.4 %slice_bitcast_fusion.1 = f32[3,80,720]{2,1,0:T(8,128)S(1)} fusion(f32[1,7,2048,80]{2,3,1,0:T(8,128)} %param.13), kind=kLoop, calls=%fused_computation.6 | loop fusion | bytes 1382400 | tf_op jit(solution)/shard_map/transpose | solution.py:325
  2.1 2.1 %collective-permute-start = (f32[40,720]{1,0:T(8,128)S(1)}, f32[40,720]{1,0:T(8,128)S(1)}, u32[]{:S(2)}, u32[]{:S(2)}) collective-permute-start(f32[40,720]{1,0:T(8,128)S(1)} %get-tuple-element.7), channel_id=1, source_target_pairs={{0,1},{1,2},{2,3},{3,4},{4,5},{5,6},{6,7},{7,0},{8,9},{9,10},{10,1... | collective-permute-start | bytes 345608 | tf_op jit(solution)/shard_map/ppermute | solution.py:330
  4.2 3.1 %collective-permute-start.1 = (f32[40,720]{1,0:T(8,128)S(1)}, f32[40,720]{1,0:T(8,128)S(1)}, u32[]{:S(2)}, u32[]{:S(2)}) collective-permute-start(f32[40,720]{1,0:T(8,128)S(1)} %get-tuple-element.8), channel_id=1, source_target_pairs={{1,0},{2,1},{3,2},{4,3},{5,4},{6,5},{7,6},{0,7},{9,8},{10,9},{11,1... | collective-permute-start | bytes 345608 | tf_op jit(solution)/shard_map/ppermute | solution.py:331
  7.3 1.1 %slice_bitcast_fusion.3 = f32[80,720]{1,0:T(8,128)S(1)} fusion(f32[10,1,2048,8]{2,3,1,0:T(8,128)} %param.14), kind=kLoop, calls=%fused_computation.21 | loop fusion | bytes 460800 | tf_op jit(solution)/shard_map/reshape | solution.py:333
  8.4 0.8 copy.22
  9.2 0.1 reshape.69
  9.3 0.8 copy.23
  10.1 0.1 reshape.70
  10.1 0.7 add_convert_fusion
  10.9 0.0 collective-permute-done
  10.9 0.0 collective-permute-done.1
  10.9 0.1 pad_maximum_fusion.1
  11.0 0.3 fusion.16
  11.2 0.7 slice_select_fusion
  11.9 0.1 fusion.6
  12.0 1.0 %pad_maximum_fusion = f32[4,248,256]{2,1,0:T(8,128)} fusion(f32[1,248,256]{2,1,0:T(8,128)S(1)} %get-tuple-element.12, f32[1,248,256]{2,1,0:T(8,128)S(1)} %get-tuple-element.11, f32[1,248,256]{2,1,0:T(8,128)S(1)} %get-tuple-element.10, f32[1,248,256]{2,1,0:T(8,128)S(1)} %get-tuple-element.9), kind=kLoop, calls=%fused_computation.3 | loop fusion | flops 761856 | bytes 2031616 | tf_op jit(solution)/shard_map/stack | solution.py:349
  13.0 5.2 %all-to-all-start = ((f32[4,248,256]{2,1,0:T(8,128)}), f32[4,248,256]{2,1,0:T(8,128)S(1)}, u32[]{:S(2)}, u32[]{:S(2)}) async-start(f32[4,248,256]{2,1,0:T(8,128)} %pad_maximum_fusion), calls=%async_computation | async-start | bytes 2031616 | tf_op jit(solution)/shard_map/all_to_all | solution.py:350
  18.3 0.7 convert_bitcast_fusion.1
  19.0 12.5 %all-to-all-done.band_ref = f32[4,248,256]{2,1,0:T(8,128)S(1)} async-done(((f32[4,248,256]{2,1,0:T(8,128)}), f32[4,248,256]{2,1,0:T(8,128)S(1)}, u32[]{:S(2)}, u32[]{:S(2)}) %all-to-all-start) | async-done | bytes 1015840 | tf_op jit(solution)/shard_map/all_to_all | solution.py:350
  31.5 0.1 fusion.17
  31.6 0.1 copy.24
  31.7 0.1 reshape.72.blk_ref
  31.8 0.1 reshape.75
  31.9 0.1 reshape.76.sy_ref
  32.0 0.1 reshape.73
  32.1 0.1 reshape.74.sx_ref
  32.2 0.0 copy-start
  32.2 0.9 copy-done
  33.1 0.0 copy-start.1
  33.1 0.9 copy-done.1
  34.0 0.0 copy-start.2
  34.0 0.8 copy-done.2
  34.9 0.0 copy-start.3
  34.9 0.8 copy-done.3
  35.7 0.0 copy-start.4
  35.7 0.8 copy-done.4
  36.5 0.0 copy-start.5
  36.5 0.7 copy-done.5
  37.2 23.0 %shard_map.140 = f32[20,2,64,128]{3,2,1,0:T(8,128)S(1)} custom-call(s32[40]{0:T(128)S(1)} %reshape.72.blk_ref, s32[240]{0:T(256)S(1)} %reshape.74.sx_ref, s32[240]{0:T(256)S(1)} %reshape.76.sy_ref, f32[4,248,256]{2,1,0:T(8,128)S(1)} %all-to-all-done.band_ref, bf16[160,240]{1,0:T(8,128)(2,1)S(1)} %copy-done.1, bf16[80,160]{1,0:T(8,128)(2,1)S(1)} %copy-done.4, ...), custom_call_target="tpu_custom_call" | custom-call | tf_op jit(solution)/shard_map/pallas_call | solution.py:191
  60.2 0.1 slice_bitcast_fusion
  60.3 0.3 copy.27
  60.7 0.4 copy.34
  61.0 1.0 copy.29
  62.0 1.6 %convert_bitcast_fusion = (bf16[10,6,20,10,2]{2,4,3,1,0:T(2,128)(2,1)S(1)}, f32[10,6,2,20,10]{3,2,4,1,0:T(2,128)}) fusion(f32[10,20]{1,0:T(8,128)S(1)} %convert_bitcast_fusion.1, f32[10,6,10,2,4]{4,3,2,1,0:T(2,128)S(1)} %copy.29, f32[10,6,10,2,16]{4,3,2,1,0:T(2,128)S(1)} %bitcast.66), kind=kLoop, calls=%fused_computation.13 | loop fusion | flops 72000 | bytes 240800 | tf_op jit(solution)/shard_map/convert_element_type | solution.py:365
  63.6 13.6 %fusion.2 = f32[10,5376]{1,0:T(8,128)S(1)} fusion(bf16[6,20,10,2,5376]{4,3,2,1,0:T(2,128)(2,1)} %bitcast.73, bf16[10,6,20,10,2]{2,4,3,1,0:T(2,128)(2,1)S(1)} %get-tuple-element.2), kind=kOutput, calls=%fused_computation.2 | convolution fusion | flops 258048000 | bytes 26067840 | tf_op jit(solution)/shard_map/dot_general | solution.py:367
  77.3 20.1 %shard_map.141 = f32[4,8,16,128]{3,2,1,0:T(8,128)S(1)} custom-call(f32[4,8,16,128]{3,2,1,0:T(8,128)S(1)} %bitcast.64), custom_call_target="tpu_custom_call" | custom-call | tf_op jit(solution)/shard_map/pallas_call | solution.py:292
  97.3 0.8 reshape.84
  (13 shorter events, 0.2 us)
Async XLA Ops:
  2.1 8.8 %collective-permute-start = (f32[40,720]{1,0:T(8,128)S(1)}, f32[40,720]{1,0:T(8,128)S(1)}, u32[]{:S(2)}, u32[]{:S(2)}) collective-permute-start(f32[40,720]{1,0:T(8,128)S(1)} %get-tuple-element.7), channel_id=1, source_target_pairs={{0,1},{1,2},{2,3},{3,4},{4,5},{5,6},{6,7},{7,0},{8,9},{9,10},{10,1... | collective-permute-start | bytes 345608 | tf_op jit(solution)/shard_map/ppermute | solution.py:330
  4.2 6.7 %collective-permute-start.1 = (f32[40,720]{1,0:T(8,128)S(1)}, f32[40,720]{1,0:T(8,128)S(1)}, u32[]{:S(2)}, u32[]{:S(2)}) collective-permute-start(f32[40,720]{1,0:T(8,128)S(1)} %get-tuple-element.8), channel_id=1, source_target_pairs={{1,0},{2,1},{3,2},{4,3},{5,4},{6,5},{7,6},{0,7},{9,8},{10,9},{11,1... | collective-permute-start | bytes 345608 | tf_op jit(solution)/shard_map/ppermute | solution.py:331
  13.0 18.5 %all-to-all-start = ((f32[4,248,256]{2,1,0:T(8,128)}), f32[4,248,256]{2,1,0:T(8,128)S(1)}, u32[]{:S(2)}, u32[]{:S(2)}) async-start(f32[4,248,256]{2,1,0:T(8,128)} %pad_maximum_fusion), calls=%async_computation | async-start | bytes 2031616 | tf_op jit(solution)/shard_map/all_to_all | solution.py:350
  32.2 0.9 copy-start
  33.1 0.9 copy-start.1
  34.0 0.8 copy-start.2
  34.9 0.8 copy-start.3
  35.7 0.8 copy-start.4
  36.5 0.7 copy-start.5

commit v3 on v2

--- a/solution.py
+++ b/solution.py
@@ -48,43 +48,48 @@
     return high, low
 
 
-def lenslet_constants(cols, used):
-    place = np.arange(PIX)
-    diff = place[:, None] - place[None, :]
-    gap = np.where(diff == 0, 1, np.abs(diff))
-    weight = -((-1.0) ** gap) / np.tan(np.pi * gap / FFT_LEN)
-    odd = np.where(diff == 0, 0.0, np.sign(diff) * weight)
-    sign = (-1.0) ** place
-    even = -0.5 * sign[:, None] * sign[None, :]
-
-    def parts(mat):
-        high = mat.astype(jnp.bfloat16)
-        return high, (mat - high.astype(np.float64)).astype(jnp.bfloat16)
-
-    odd_c = np.kron(np.eye(cols // PIX), odd)
-    even_c = np.kron(np.eye(cols // PIX), even).astype(jnp.bfloat16)
-    high, low = parts(odd_c)
-    zero = np.zeros_like(high)
-    left_c = np.concatenate(
-        [np.concatenate([high, high, low], 1), np.concatenate([even_c, even_c, zero], 1)], 0
-    )
-    left_s = np.concatenate([even_c, even_c], 1)
-    high, low = parts(np.kron(np.eye(LANES // PIX), odd.T))
-    even_r = np.kron(np.eye(LANES // PIX), even).astype(jnp.bfloat16)
-    zero = np.zeros_like(high)
-    right_c = np.concatenate(
-        [np.concatenate([high, low], 1), np.concatenate([high, zero], 1)], 0
-    )
-    right_e = np.concatenate([even_r, even_r], 0)
-    sum_l = np.zeros((SUBS, cols))
-    for c in range(used):
-        sum_l[c // PIX, c] = 1.0
-    sum_l = np.concatenate([sum_l, sum_l], 1).astype(jnp.bfloat16)
-    sum_r = np.zeros((LANES, LANES))
-    for c in range(LANES):
-        sum_r[c, c // PIX] = 1.0
-    sum_r = np.concatenate([sum_r, sum_r], 0).astype(jnp.bfloat16)
-    return [jnp.asarray(m) for m in (left_c, left_s, right_c, right_e, sum_l, sum_r)]
+def lattice(shape):
+    return tuple(lax.broadcasted_iota(jnp.int32, shape, axis) for axis in (0, 1))
+
+
+def odd_form(row, col):
+    gap = row - col
+    value = jnp.zeros(row.shape, jnp.float32)
+    for d in range(1, PIX):
+        weight = np.float32(-((-1.0) ** d) / math.tan(math.pi * d / FFT_LEN))
+        value = jnp.where(gap == d, weight, jnp.where(gap == -d, -weight, value))
+    return jnp.where((row >> 3) == (col >> 3), value, 0.0)
+
+
+def even_form(row, col):
+    value = jnp.where(((row + col) & 1) == 1, np.float32(0.5), np.float32(-0.5))
+    return jnp.where((row >> 3) == (col >> 3), value, 0.0)
+
+
+def fill_constants(cols, used, left_c, left_s, right_c, right_e, sum_l, sum_r):
+    row, col = lattice((cols, 3 * cols))
+    third = col >= 2 * cols
+    inner = col - jnp.where(third, 2 * cols, jnp.where(col >= cols, cols, 0))
+    value = odd_form(row, inner)
+    high = value.astype(jnp.bfloat16).astype(jnp.float32)
+    left_c[0:cols, :] = jnp.where(third, value - high, high).astype(jnp.bfloat16)
+    left_c[cols:, :] = jnp.where(third, 0.0, even_form(row, inner)).astype(jnp.bfloat16)
+    row, col = lattice((cols, 2 * cols))
+    inner = col - jnp.where(col >= cols, cols, 0)
+    left_s[...] = even_form(row, inner).astype(jnp.bfloat16)
+    row, col = lattice((2 * LANES, 2 * LANES))
+    value = odd_form(col & (LANES - 1), row & (LANES - 1))
+    high = value.astype(jnp.bfloat16).astype(jnp.float32)
+    low = jnp.where(row < LANES, value - high, 0.0)
+    right_c[...] = jnp.where(col < LANES, high, low).astype(jnp.bfloat16)
+    row, col = lattice((2 * LANES, LANES))
+    row = row & (LANES - 1)
+    right_e[...] = even_form(row, col).astype(jnp.bfloat16)
+    sum_r[...] = jnp.where((row >> 3) == col, 1.0, 0.0).astype(jnp.bfloat16)
+    row, col = lattice((SUBS, 2 * cols))
+    inner = col - jnp.where(col >= cols, cols, 0)
+    inside = ((inner >> 3) == row) & (inner < used)
+    sum_l[...] = jnp.where(inside, 1.0, 0.0).astype(jnp.bfloat16)
 
 
 def mm(a, b):
@@ -92,10 +97,9 @@
 
 
 def lenslet_kernel(
-    layers, stars, rows, cols, ext,
-    blk_ref, sx_ref, sy_ref, band_ref,
+    layers, stars, rows, cols, used,
+    blk_ref, sx_ref, sy_ref, band_ref, out_ref, screen_ref,
     left_c_ref, left_s_ref, right_c_ref, right_e_ref, sum_l_ref, sum_r_ref,
-    out_ref, screen_ref,
 ):
     main = rows // LANES
     rem = rows % LANES
@@ -103,16 +107,27 @@
     groups = stars // GROUP
     lane = lax.broadcasted_iota(jnp.int32, (cols, LANES), 1)
 
+    fill_constants(
+        cols, used, left_c_ref, left_s_ref, right_c_ref, right_e_ref, sum_l_ref, sum_r_ref
+    )
+    rims = band_ref.shape[1] - 2 * HALO
     for l in range(layers):
         for j in range(tiles):
-            screen_ref[l, j, 0:ext, :] = band_ref[l, 0:ext, j * LANES : (j + 1) * LANES]
+            cut = slice(j * LANES, (j + 1) * LANES)
+            screen_ref[l, j, 0:HALO, :] = band_ref[l, rims : rims + HALO, cut]
+            screen_ref[l, j, HALO : HALO + used, :] = band_ref[l, 0:used, cut]
+            screen_ref[l, j, HALO + used : 2 * HALO + used, :] = band_ref[l, rims + HALO :, cut]
+            if cols > used:
+                screen_ref[l, j, 2 * HALO + used : 2 * HALO + cols, :] = jnp.zeros(
+                    (cols - used, LANES), jnp.float32
+                )
 
     def body(i, carry):
         t = i // groups
         h = i % groups
         for l in range(layers):
             start = pl.multiple_of(blk_ref[t * layers + l] * NEW_COLS, NEW_COLS)
-            row = pl.multiple_of(ext + t * NEW_COLS, NEW_COLS)
+            row = pl.multiple_of(used + t * NEW_COLS, NEW_COLS)
             for j in range(tiles):
                 screen_ref[l, j, pl.ds(start, NEW_COLS), :] = band_ref[
                     l, pl.ds(row, NEW_COLS), j * LANES : (j + 1) * LANES
@@ -177,7 +192,7 @@
         out_ref[i, 1] = every[size : 2 * size] / total
         return carry
 
-    lax.fori_loop(0, blk_ref.shape[0] // layers * groups, body, 0)
+    lax.fori_loop(0, blk_ref.shape[0] // layers * groups, body, 0, unroll=2)
 
 
 def lenslet_slopes(band, blocks, step_x, step_y, rows, cols, ext, interpret=False):
@@ -189,19 +204,22 @@
     smem = pl.BlockSpec(memory_space=pltpu.SMEM)
     vmem = pl.BlockSpec(memory_space=pltpu.VMEM)
     out = pl.pallas_call(
-        functools.partial(lenslet_kernel, layers, stars, rows, padded, ext),
+        functools.partial(lenslet_kernel, layers, stars, rows, padded, cols),
         out_shape=jax.ShapeDtypeStruct((steps * groups, 2, tiles * SUBS, LANES), jnp.float32),
-        in_specs=[smem] * 3 + [vmem] * 7,
+        in_specs=[smem] * 3 + [vmem],
         out_specs=vmem,
         scratch_shapes=[
-            pltpu.VMEM((layers, band.shape[2] // LANES, ext + NEW_COLS, LANES), jnp.float32)
+            pltpu.VMEM((layers, band.shape[2] // LANES, ext + NEW_COLS, LANES), jnp.float32),
+            pltpu.VMEM((2 * padded, 3 * padded), jnp.bfloat16),
+            pltpu.VMEM((padded, 2 * padded), jnp.bfloat16),
+            pltpu.VMEM((2 * LANES, 2 * LANES), jnp.bfloat16),
+            pltpu.VMEM((2 * LANES, LANES), jnp.bfloat16),
+            pltpu.VMEM((SUBS, 2 * padded), jnp.bfloat16),
+            pltpu.VMEM((2 * LANES, LANES), jnp.bfloat16),
         ],
         compiler_params=pltpu.CompilerParams(vmem_limit_bytes=40 * 1024 * 1024),
         interpret=interpret,
-    )(
-        blocks.reshape(-1), step_x.reshape(-1), step_y.reshape(-1), band,
-        *lenslet_constants(padded, cols),
-    )
+    )(blocks.reshape(-1), step_x.reshape(-1), step_y.reshape(-1), band)
     out = out.reshape(steps, groups, 2, tiles, SUBS, LANES)[:, :, :, :, : cols // PIX]
     found = []
     if main:
@@ -310,6 +328,62 @@
     return total.reshape(-1, LANES)[:lines].reshape(part.shape)
 
 
+def exchange_kernel(sent_ref, got_ref, send, recv):
+    layers = sent_ref.shape[0]
+    rims = sent_ref.shape[1] - 2 * HALO
+    me_l = lax.axis_index("layer")
+    me_s = lax.axis_index("sub")
+    subs = lax.axis_size("sub")
+    right = lax.rem(me_s + 1, subs)
+    left = lax.rem(me_s + subs - 1, subs)
+    mesh_id = pl.DeviceIdType.MESH
+    peers = [lax.rem(me_l + j, layers) for j in range(layers)]
+
+    barrier = pltpu.get_barrier_semaphore()
+    for p in peers[1:]:
+        pl.semaphore_signal(barrier, inc=1, device_id=(p, me_s), device_id_type=mesh_id)
+    for p in peers:
+        for side in (right, left):
+            pl.semaphore_signal(barrier, inc=1, device_id=(p, side), device_id_type=mesh_id)
+    pl.semaphore_wait(barrier, 3 * layers - 1)
+
+    copies = []
+
+    def push(p, side, start, size):
+        at = pl.ds(start, size)
+        copy = pltpu.make_async_remote_copy(
+            src_ref=sent_ref.at[p, at], dst_ref=got_ref.at[me_l, at],
+            send_sem=send.at[len(copies)], recv_sem=recv.at[len(copies)],
+            device_id=(p, side), device_id_type=mesh_id,
+        )
+        copy.start()
+        copies.append(copy)
+
+    for p in peers[1:]:
+        push(p, me_s, 0, rims)
+    for p in peers:
+        push(p, right, rims, HALO)
+        push(p, left, rims + HALO, HALO)
+    got_ref[me_l, 0:rims] = sent_ref[me_l, 0:rims]
+    for copy in copies:
+        copy.wait()
+
+
+def exchanged(sent):
+    vmem = pl.BlockSpec(memory_space=pltpu.VMEM)
+    count = 3 * sent.shape[0] - 1
+    return pl.pallas_call(
+        exchange_kernel,
+        out_shape=jax.ShapeDtypeStruct(sent.shape, sent.dtype),
+        in_specs=[vmem],
+        out_specs=vmem,
+        scratch_shapes=[pltpu.SemaphoreType.DMA((count,)), pltpu.SemaphoreType.DMA((count,))],
+        compiler_params=pltpu.CompilerParams(
+            collective_id=1, has_side_effects=True, vmem_limit_bytes=32 * 1024 * 1024
+        ),
+    )(sent)
+
+
 def local(screens, new_columns, col_block, shift_x, shift_y, valid, recon):
     width = screens.shape[3]
     steps, _, stars = shift_x.shape
@@ -325,31 +399,24 @@
     band = jnp.transpose(band, (0, 2, 1))
     tail = jnp.where(owner == subs - 1, band[0, width - HALO :], band[1, width - HALO :])
     head = jnp.where(owner == 0, band[2, :HALO], band[1, :HALO])
-    forward = [(i, (i + 1) % subs) for i in range(subs)]
-    backward = [(b, a) for a, b in forward]
-    before = lax.ppermute(tail, "sub", forward)
-    after = lax.ppermute(head, "sub", backward)
     fresh = jnp.transpose(new_columns[:, 0, ROW0 - HALO : ROW0 + PUP + HALO, :], (0, 2, 1))
     fresh = fresh.reshape(steps * NEW_COLS, PUP + 2 * HALO)
-    pieces = [before, band[1], after]
-    if cols > width:
-        pieces.append(jnp.zeros((cols - width, PUP + 2 * HALO), jnp.float32))
-    strip = jnp.concatenate(pieces + [fresh], axis=0)
+    strip = jnp.concatenate([band[1], fresh, jnp.zeros((8, band.shape[2])), tail, head], axis=0)
     plan = jnp.concatenate(
         [col_block.reshape(-1), shift_x.reshape(-1), shift_y.reshape(-1)]
     ).astype(jnp.float32)
     lines = -(-plan.shape[0] // lanes)
     plan = jnp.pad(plan, (0, 8 * lanes - plan.shape[0])).reshape(8, lanes)
 
+    last = width + steps * NEW_COLS
+
     def share(i):
         cut = strip[:, i * rows : i * rows + rows + 2 * HALO]
         cut = jnp.pad(cut, ((0, 0), (0, lanes - cut.shape[1])))
-        return jnp.concatenate([cut, plan], axis=0)
-
-    sent = jnp.stack([share(i) for i in range(count)])
-    got = lax.all_to_all(sent, "layer", split_axis=0, concat_axis=0, tiled=True)
-
-    last = ext + steps * NEW_COLS
+        return cut.at[last : last + 8].set(plan)
+
+    got = exchanged(jnp.stack([share(i) for i in range(count)]))
+
     plans = got[:, last : last + lines].reshape(count, -1).astype(jnp.int32)
     blocks = plans[:, :steps].T
     step_x = plans[:, steps : steps + steps * stars].reshape(count, steps, stars)

time: 98.8 us -> 82.5 us (0.84)
  Pallas kernels: 43.1 us -> 56.1 us
  waiting for transfers between devices: 12.6 us -> 0 us
  starting transfers between devices: 10.5 us -> 0 us
  local copies, waits for them, and re-layouts: 12.7 us -> 7.84 us
  other arithmetic: 4.9 us -> 3.88 us
    pallas_call x0 -> x1, Pallas kernels: none -> 17.2 us  [exchanged(): pl.pallas_call(exchange_kernel, out_shape=jax.ShapeDtypeStruct(sent.shape...]
    all_to_all x1 -> x0, waiting for transfers between devices: 12.5 us -> none  [local(): got = lax.all_to_all(sent, 'layer', split_axis=0, concat_axis=0, tiled=True)]
    all_to_all x1 -> x0, starting transfers between devices: 5.25 us -> none  [local(): got = lax.all_to_all(sent, 'layer', split_axis=0, concat_axis=0, tiled=True)]
    ppermute x2 -> x0, starting transfers between devices: 5.23 us -> none  [the longest x1 3.1 us: local(): after = lax.ppermute(head, 'sub', backward)]
    pallas_call x1, Pallas kernels: 23 us -> 18.9 us  [lenslet_slopes(): pl.pallas_call(functools.partial(lenslet_kernel, layers, stars, rows, pad...]
    unnamed x16 -> x7, local copies, waits for them, and re-layouts: 6.86 us -> 3.01 us
    reshape x2 -> x0, local copies, waits for them, and re-layouts: 1.09 us -> none  [the longest x1 1.08 us: local(): fresh = fresh.reshape(steps * NEW_COLS, PUP + 2 * HALO)]
  transfers between devices with their start and end apart: 3 -> 0, of which waited for: 1 -> 0; matrix products, arithmetic and copies ran while one was open for 4% -> 0% of each run, Pallas kernels for 0% -> 0%
where the time goes in v3:
time: 82.5 us; the launch traced here: 82.2 us
  Pallas kernels  56.1 us (68%)
  matrix products  13.6 us (16%)
  local copies, waits for them, and re-layouts  7.84 us (10%)
  other arithmetic  3.88 us (5%)
    pallas_call x1, Pallas kernels, summed_everywhere(): pl.pallas_call(sum_kernel, out_shape=jax.ShapeDtypeStruct(padded.shape, j...  20 us
    pallas_call x1, Pallas kernels, lenslet_slopes(): pl.pallas_call(functools.partial(lenslet_kernel, layers, stars, rows, pad...  18.9 us
    pallas_call x1, Pallas kernels, exchanged(): pl.pallas_call(exchange_kernel, out_shape=jax.ShapeDtypeStruct(sent.shape...  17.2 us
    dot_general x1, matrix products, local(): part = jnp.dot(flat, matrix, preferred_element_type=jnp.float32)  13.6 us
    unnamed x7, local copies, waits for them, and re-layouts  3.01 us

profile of v3, /device:TPU:1, one launch (start us, length us, event | category | flops | bytes accessed | tf_op | source)
XLA Modules:
  0.0 82.2 jit_solution(647004013445120913)
XLA Ops:
  0.6 0.8 copy.16
  1.4 0.1 reshape.168
  1.5 0.8 copy.17
  2.3 0.1 reshape.169
  2.4 0.7 add_convert_fusion
  3.1 0.7 convert_bitcast_fusion.1
  3.8 1.4 %slice_bitcast_fusion.1 = f32[3,80,720]{2,1,0:T(8,128)S(1)} fusion(f32[1,7,2048,80]{2,3,1,0:T(8,128)} %param.15), kind=kLoop, calls=%fused_computation.5 | loop fusion | bytes 1382400 | tf_op jit(solution)/shard_map/transpose | solution.py:399
  5.2 1.1 %bitcast_dynamic-update-slice_fusion = f32[248,720]{1,0:T(8,128)S(1)} fusion(f32[248,720]{1,0:T(8,128)S(1)} %fusion.7, f32[10,1,2048,8]{2,3,1,0:T(8,128)} %param.16), kind=kLoop, calls=%fused_computation.16 | loop fusion | bytes 476160
  6.4 0.3 fusion.16
  6.7 0.7 fusion.6
  7.4 0.1 pad_bitcast_fusion
  7.4 0.1 pad_maximum_fusion.sent_ref
  7.5 17.2 %shard_map.86.band_ref = f32[4,248,256]{2,1,0:T(8,128)S(1)} custom-call(f32[4,248,256]{2,1,0:T(8,128)S(1)} %pad_maximum_fusion.sent_ref), custom_call_target="tpu_custom_call" | custom-call | tf_op jit(solution)/shard_map/pallas_call | solution.py:375
  24.8 0.1 fusion.17
  24.9 0.1 copy.18
  25.0 0.1 reshape.170.blk_ref
  25.0 0.1 reshape.173
  25.1 0.1 reshape.174.sy_ref
  25.3 0.1 reshape.171
  25.4 0.1 reshape.172.sx_ref
  25.5 18.9 %shard_map.87 = f32[20,2,64,128]{3,2,1,0:T(8,128)S(1)} custom-call(s32[40]{0:T(128)S(1)} %reshape.170.blk_ref, s32[240]{0:T(256)S(1)} %reshape.172.sx_ref, s32[240]{0:T(256)S(1)} %reshape.174.sy_ref, f32[4,248,256]{2,1,0:T(8,128)S(1)} %shard_map.86.band_ref), custom_call_target="tpu_custom_call" | custom-call | tf_op jit(solution)/shard_map/pallas_call | solution.py:206
  44.4 0.1 slice_bitcast_fusion
  44.5 0.3 copy.21
  44.8 0.4 copy.28
  45.2 1.0 %copy.23 = f32[10,6,10,2,4]{4,3,2,1,0:T(2,128)S(1)} copy(f32[10,6,10,2,4]{2,3,4,1,0:T(2,128)S(1)} %bitcast.73) | data formatting | bytes 38400 | tf_op jit(solution)/shard_map/reshape | solution.py:235
  46.1 1.6 %convert_bitcast_fusion = (bf16[10,6,20,10,2]{2,4,3,1,0:T(2,128)(2,1)S(1)}, f32[10,6,2,20,10]{3,2,4,1,0:T(2,128)}) fusion(f32[10,20]{1,0:T(8,128)S(1)} %convert_bitcast_fusion.1, f32[10,6,10,2,4]{4,3,2,1,0:T(2,128)S(1)} %copy.23, f32[10,6,10,2,16]{4,3,2,1,0:T(2,128)S(1)} %bitcast.72), kind=kLoop, calls=%fused_computation.8 | loop fusion | flops 72000 | bytes 240800 | tf_op jit(solution)/shard_map/convert_element_type | solution.py:432
  47.7 13.6 %fusion.2 = f32[10,5376]{1,0:T(8,128)S(1)} fusion(bf16[6,20,10,2,5376]{4,3,2,1,0:T(2,128)(2,1)} %bitcast.79, bf16[10,6,20,10,2]{2,4,3,1,0:T(2,128)(2,1)S(1)} %get-tuple-element.50), kind=kOutput, calls=%fused_computation.2 | convolution fusion | flops 258048000 | bytes 26067840 | tf_op jit(solution)/shard_map/dot_general | solution.py:434
  61.4 20.0 %shard_map.88 = f32[4,8,16,128]{3,2,1,0:T(8,128)S(1)} custom-call(f32[4,8,16,128]{3,2,1,0:T(8,128)S(1)} %bitcast.70), custom_call_target="tpu_custom_call" | custom-call | tf_op jit(solution)/shard_map/pallas_call | solution.py:310
  81.4 0.8 reshape.182
  (16 shorter events, 0.2 us)

commit v4 on v3

--- a/solution.py
+++ b/solution.py
@@ -288,13 +288,15 @@
     copies = [
         push(own, own, send_3, recv_3, j, (me_l, q)) for j, q in enumerate(sub_peers)
     ]
-    for copy in copies:
-        copy.wait()
-    own = out_ref.at[me_l]
-    copies = [
-        push(own, own, send_4, recv_4, j, (p, me_s)) for j, p in enumerate(layer_peers)
-    ]
-    for copy in copies:
+    for j in range(subs):
+        if j:
+            copies[j - 1].wait()
+        own = out_ref.at[me_l, lax.rem(me_s + subs - j, subs)]
+        copies.extend(
+            push(own, own, send_4, recv_4, j * (layers - 1) + i, (p, me_s))
+            for i, p in enumerate(layer_peers)
+        )
+    for copy in copies[subs - 1 :]:
         copy.wait()
 
 
@@ -319,7 +321,7 @@
             dma((layers - 1,)), dma((layers - 1,)),
             dma((subs - 1,)), dma((subs - 1,)),
             dma((subs - 1,)), dma((subs - 1,)),
-            dma((layers - 1,)), dma((layers - 1,)),
+            dma((subs * (layers - 1),)), dma((subs * (layers - 1),)),
         ],
         compiler_params=pltpu.CompilerParams(
             collective_id=0, has_side_effects=True, vmem_limit_bytes=32 * 1024 * 1024

time: 82.5 us -> 83.3 us (level)
  no operation moved by 1% of the time
where the time goes in v4:
time: 83.3 us; the launch traced here: 82.6 us
  Pallas kernels  56.4 us (68%)
  matrix products  13.6 us (16%)
  local copies, waits for them, and re-layouts  7.84 us (9%)
  other arithmetic  3.88 us (5%)
    pallas_call x1, Pallas kernels, summed_everywhere(): pl.pallas_call(sum_kernel, out_shape=jax.ShapeDtypeStruct(padded.shape, j...  20.4 us
    pallas_call x1, Pallas kernels, lenslet_slopes(): pl.pallas_call(functools.partial(lenslet_kernel, layers, stars, rows, pad...  18.8 us
    pallas_call x1, Pallas kernels, exchanged(): pl.pallas_call(exchange_kernel, out_shape=jax.ShapeDtypeStruct(sent.shape...  17.2 us
    dot_general x1, matrix products, local(): part = jnp.dot(flat, matrix, preferred_element_type=jnp.float32)  13.6 us
    unnamed x7, local copies, waits for them, and re-layouts  3.01 us

profile of v4, /device:TPU:1, one launch (start us, length us, event | category | flops | bytes accessed | tf_op | source)
XLA Modules:
  0.0 82.6 jit_solution(13993288512033802095)
XLA Ops:
  0.6 0.8 copy.16
  1.4 0.1 reshape.168
  1.5 0.8 copy.17
  2.3 0.1 reshape.169
  2.4 0.7 add_convert_fusion
  3.1 0.7 convert_bitcast_fusion.1
  3.8 1.4 %slice_bitcast_fusion.1 = f32[3,80,720]{2,1,0:T(8,128)S(1)} fusion(f32[1,7,2048,80]{2,3,1,0:T(8,128)} %param.15), kind=kLoop, calls=%fused_computation.5 | loop fusion | bytes 1382400 | tf_op jit(solution)/shard_map/transpose | solution.py:401
  5.2 1.1 %bitcast_dynamic-update-slice_fusion = f32[248,720]{1,0:T(8,128)S(1)} fusion(f32[248,720]{1,0:T(8,128)S(1)} %fusion.7, f32[10,1,2048,8]{2,3,1,0:T(8,128)} %param.16), kind=kLoop, calls=%fused_computation.16 | loop fusion | bytes 476160
  6.4 0.3 fusion.16
  6.7 0.7 fusion.6
  7.4 0.1 pad_bitcast_fusion
  7.4 0.1 pad_maximum_fusion.sent_ref
  7.5 17.2 %shard_map.86.band_ref = f32[4,248,256]{2,1,0:T(8,128)S(1)} custom-call(f32[4,248,256]{2,1,0:T(8,128)S(1)} %pad_maximum_fusion.sent_ref), custom_call_target="tpu_custom_call" | custom-call | tf_op jit(solution)/shard_map/pallas_call | solution.py:377
  24.8 0.1 fusion.17
  24.9 0.1 copy.18
  25.0 0.1 reshape.170.blk_ref
  25.0 0.1 reshape.173
  25.1 0.1 reshape.174.sy_ref
  25.3 0.1 reshape.171
  25.4 0.1 reshape.172.sx_ref
  25.5 18.8 %shard_map.87 = f32[20,2,64,128]{3,2,1,0:T(8,128)S(1)} custom-call(s32[40]{0:T(128)S(1)} %reshape.170.blk_ref, s32[240]{0:T(256)S(1)} %reshape.172.sx_ref, s32[240]{0:T(256)S(1)} %reshape.174.sy_ref, f32[4,248,256]{2,1,0:T(8,128)S(1)} %shard_map.86.band_ref), custom_call_target="tpu_custom_call" | custom-call | tf_op jit(solution)/shard_map/pallas_call | solution.py:206
  44.4 0.1 slice_bitcast_fusion
  44.5 0.3 copy.21
  44.8 0.4 copy.28
  45.2 1.0 %copy.23 = f32[10,6,10,2,4]{4,3,2,1,0:T(2,128)S(1)} copy(f32[10,6,10,2,4]{2,3,4,1,0:T(2,128)S(1)} %bitcast.73) | data formatting | bytes 38400 | tf_op jit(solution)/shard_map/reshape | solution.py:235
  46.1 1.6 %convert_bitcast_fusion = (bf16[10,6,20,10,2]{2,4,3,1,0:T(2,128)(2,1)S(1)}, f32[10,6,2,20,10]{3,2,4,1,0:T(2,128)}) fusion(f32[10,20]{1,0:T(8,128)S(1)} %convert_bitcast_fusion.1, f32[10,6,10,2,4]{4,3,2,1,0:T(2,128)S(1)} %copy.23, f32[10,6,10,2,16]{4,3,2,1,0:T(2,128)S(1)} %bitcast.72), kind=kLoop, calls=%fused_computation.8 | loop fusion | flops 72000 | bytes 240800 | tf_op jit(solution)/shard_map/convert_element_type | solution.py:434
  47.7 13.6 %fusion.2 = f32[10,5376]{1,0:T(8,128)S(1)} fusion(bf16[6,20,10,2,5376]{4,3,2,1,0:T(2,128)(2,1)} %bitcast.79, bf16[10,6,20,10,2]{2,4,3,1,0:T(2,128)(2,1)S(1)} %get-tuple-element.50), kind=kOutput, calls=%fused_computation.2 | convolution fusion | flops 258048000 | bytes 26067840 | tf_op jit(solution)/shard_map/dot_general | solution.py:436
  61.4 20.4 %shard_map.88 = f32[4,8,16,128]{3,2,1,0:T(8,128)S(1)} custom-call(f32[4,8,16,128]{3,2,1,0:T(8,128)S(1)} %bitcast.70), custom_call_target="tpu_custom_call" | custom-call | tf_op jit(solution)/shard_map/pallas_call | solution.py:312
  81.8 0.8 reshape.182
  (16 shorter events, 0.2 us)
